TPU v7x, 512 devices: a whole 4x8x8 slice. The times are simulated.
512 devices in a mesh: gx: 32 (over z, y_hi), gy: 16 (over x, y_lo, core).
Axes of the slice: x: 4, y: 8 (y_hi: 4, y_lo: 2; y = y_hi * 2 + y_lo), z: 8, core: 2. Of those that a mesh axis runs over, the one named last changes fastest.
Arguments:
- transfer: bfloat16 [32, 16, 2, 1024, 1024], P('gx', 'gy'), may hold values from -0.09375 to 0.09375
- sources: bfloat16 [32, 16, 2, 64, 1024], P('gx', 'gy'), may hold values from -6 to 6
- quad_nodes: int32 [8], replicated, may hold values from 0 to 7, each once
Outputs:
- outgoing: bfloat16 [32, 16, 2, 64, 1024], P('gx', 'gy')
Inputs may be any that keep to these rules, and one draw needn't show every extreme that they name: `quad_nodes`: each node is used by exactly one block.
All inputs are finite; a program needn't handle non-finite values.
Results may differ from a plain program's by a relative error of at most 0.017.
Values may be sent and summed in bfloat16 or wider, within the bound.
A program may use at most 64 MiB of HBM per device.

v0:
```python
import math

import jax
import jax.numpy as jnp
from jax import lax
from jax.sharding import PartitionSpec as P

SPANS = 8
SECTIONS = 8


def shifted(block, axis, distance):
    devices = range(lax.axis_size(axis))
    route = [(i - distance, i) for i in devices if i - distance in devices]
    return lax.ppermute(block, axis, route)


def apply_block(driven, weights, sig_re, sig_im):
    u_re, u_im = (driven[0], driven[1])
    w_re = weights[0]
    w_im = weights[1]
    real_part = jnp.dot(u_re, w_re, preferred_element_type=jnp.float32) - jnp.dot(
        u_im, w_im, preferred_element_type=jnp.float32
    )
    imag_part = jnp.dot(u_re, w_im, preferred_element_type=jnp.float32) + jnp.dot(
        u_im, w_re, preferred_element_type=jnp.float32
    )
    f_re = u_re.astype(jnp.float32)
    f_im = u_im.astype(jnp.float32)
    real_part = real_part + sig_re * f_re - sig_im * f_im
    imag_part = imag_part + sig_re * f_im + sig_im * f_re
    return jnp.stack([real_part, imag_part]).astype(jnp.bfloat16)


def per_device(transfer, sources, quad_nodes):
    weights = transfer[0, 0]
    source = sources[0, 0]
    row_count = source.shape[1]
    order_cells = source.shape[2]
    edge_cells = order_cells // 2
    block_rows = row_count // SPANS
    angles = math.pi * (quad_nodes.astype(jnp.float32) + 0.5) / SPANS
    sig_re = jnp.repeat(0.5 * jnp.cos(angles), block_rows)[:, None]
    sig_im = jnp.repeat(0.5 * jnp.sin(angles), block_rows)[:, None]
    incoming = jnp.zeros(source.shape, jnp.bfloat16)
    outgoing = incoming
    for section_index in range(SECTIONS):
        driven = (incoming.astype(jnp.float32) + source.astype(jnp.float32)).astype(jnp.bfloat16)
        sending = section_index + 1 < SECTIONS
        outgoing = apply_block(driven, weights, sig_re, sig_im)
        if sending:
            in_left = shifted(outgoing[..., :edge_cells], "gx", 1)
            in_bottom = shifted(outgoing[..., edge_cells:], "gy", 1)
            incoming = jnp.concatenate([in_left, in_bottom], axis=-1)
    return outgoing[None, None]


def solution(mesh):
    placed = (P("gx", "gy", None, None, None), P("gx", "gy", None, None, None), P())
    return jax.shard_map(
        per_device,
        mesh=mesh,
        in_specs=placed,
        out_specs=P("gx", "gy", None, None, None),
        check_vma=False,
    )
```

profile of v0, /device:TPU:264, one launch (start us, length us, event | category | flops | bytes accessed | tf_op | source)
XLA Modules:
  0.0 115.3 jit_solution(15688509782776526643)
XLA Ops:
  0.0 2.2 %fusion.28 = f32[64,1024]{1,0:T(8,128)S(1)} fusion(bf16[1,1,2,64,1024]{4,3,2,1,0:T(8,128)(2,1)} %param.4, bf16[1,1,2,1024,1024]{4,3,2,1,0:T(8,128)(2,1)} %param.3), kind=kOutput, calls=%fused_computation.28 | convolution fusion | flops 134217728 | bytes 2490368 | tf_op jit(solution)/shard_map/dot_general | solution.py:25
  2.2 2.1 %fusion.30 = f32[64,1024]{1,0:T(8,128)S(1)} fusion(bf16[1,1,2,64,1024]{4,3,2,1,0:T(8,128)(2,1)} %param.4, bf16[1,1,2,1024,1024]{4,3,2,1,0:T(8,128)(2,1)} %param.3), kind=kOutput, calls=%fused_computation.30 | convolution fusion | flops 134217728 | bytes 2490368 | tf_op jit(solution)/shard_map/dot_general | solution.py:22
  4.4 0.1 broadcast_in_dim.8
  4.5 0.1 mul.77
  4.6 0.1 broadcast_in_dim.9
  4.6 0.1 mul.81
  4.7 2.3 %fusion.259 = bf16[1,64,1024]{2,1,0:T(8,128)(2,1)S(1)} fusion(f32[64,1024]{1,0:T(8,128)S(1)} %fusion.28, f32[64]{0:T(128)S(1)} %mul.81, f32[64]{0:T(128)S(1)} %mul.77, bf16[1,1,2,64,1024]{4,3,2,1,0:T(8,128)(2,1)S(1)} %copy-done, bf16[1,1,2,1024,1024]{4,3,2,1,0:T(8,128)(2,1)} %param.3), kind=kOutput, calls=%fused_computation.136 | convolution fusion | flops 134742016 | bytes 2884608 | tf_op jit(solution)/shard_map/dot_general | solution.py:25
  7.0 2.1 %fusion.256 = bf16[1,64,1024]{2,1,0:T(8,128)(2,1)S(1)} fusion(f32[64,1024]{1,0:T(8,128)S(1)} %fusion.30, f32[64]{0:T(128)S(1)} %mul.81, f32[64]{0:T(128)S(1)} %mul.77, bf16[1,1,2,64,1024]{4,3,2,1,0:T(8,128)(2,1)S(1)} %copy-done, bf16[1,1,2,1024,1024]{4,3,2,1,0:T(8,128)(2,1)} %param.3), kind=kOutput, calls=%fused_computation.135 | convolution fusion | flops 134742016 | bytes 2884608 | tf_op jit(solution)/shard_map/dot_general | solution.py:22
  9.2 4.5 %collective-permute-start = (bf16[2,64,512]{2,1,0:T(8,128)(2,1)S(1)}, bf16[2,64,512]{2,1,0:T(8,128)(2,1)S(1)}, u32[]{:S(2)}, u32[]{:S(2)}) collective-permute-start(bf16[2,64,512]{2,1,0:T(8,128)(2,1)S(1)} %get-tuple-element.17), channel_id=1, source_target_pairs={{0,16},{16,32},{32,48},{48,64},{64,80},{80,96},{96,112},{112,128},... | collective-permute-start | bytes 393224 | tf_op jit(solution)/shard_map/ppermute | solution.py:15
  13.7 1.9 %collective-permute-start.1 = (bf16[2,64,512]{2,1,0:T(8,128)(2,1)S(1)}, bf16[2,64,512]{2,1,0:T(8,128)(2,1)S(1)}, u32[]{:S(2)}, u32[]{:S(2)}) collective-permute-start(bf16[2,64,512]{2,1,0:T(8,128)(2,1)S(1)} %get-tuple-element.18), channel_id=1, source_target_pairs={{0,1},{1,2},{2,3},{3,4},{4,5},{5,6},{6,7},{7,8},{8,9},{9,10},{10,1... | collective-permute-start | bytes 393224 | tf_op jit(solution)/shard_map/ppermute | solution.py:15
  15.6 7.6 %collective-permute-done = bf16[2,64,512]{2,1,0:T(8,128)(2,1)S(1)} collective-permute-done((bf16[2,64,512]{2,1,0:T(8,128)(2,1)S(1)}, bf16[2,64,512]{2,1,0:T(8,128)(2,1)S(1)}, u32[]{:S(2)}, u32[]{:S(2)}) %collective-permute-start) | collective-permute-done | bytes 131104 | tf_op jit(solution)/shard_map/ppermute | solution.py:15
  23.2 0.1 fusion.304
  23.3 0.5 fusion.24
  23.8 0.5 fusion.26
  24.3 0.5 fusion.265
  24.8 0.5 fusion.262
  25.4 4.0 %collective-permute-start.2 = (bf16[2,64,512]{2,1,0:T(8,128)(2,1)S(1)}, bf16[2,64,512]{2,1,0:T(8,128)(2,1)S(1)}, u32[]{:S(2)}, u32[]{:S(2)}) collective-permute-start(bf16[2,64,512]{2,1,0:T(8,128)(2,1)S(1)} %get-tuple-element.15), channel_id=1, source_target_pairs={{0,16},{16,32},{32,48},{48,64},{64,80},{80,96},{96,112},{112,128},... | collective-permute-start | bytes 393224 | tf_op jit(solution)/shard_map/ppermute | solution.py:15
  29.3 1.9 %collective-permute-start.3 = (bf16[2,64,512]{2,1,0:T(8,128)(2,1)S(1)}, bf16[2,64,512]{2,1,0:T(8,128)(2,1)S(1)}, u32[]{:S(2)}, u32[]{:S(2)}) collective-permute-start(bf16[2,64,512]{2,1,0:T(8,128)(2,1)S(1)} %get-tuple-element.16), channel_id=1, source_target_pairs={{0,1},{1,2},{2,3},{3,4},{4,5},{5,6},{6,7},{7,8},{8,9},{9,10},{10,1... | collective-permute-start | bytes 393224 | tf_op jit(solution)/shard_map/ppermute | solution.py:15
  31.3 7.0 %collective-permute-done.2 = bf16[2,64,512]{2,1,0:T(8,128)(2,1)S(1)} collective-permute-done((bf16[2,64,512]{2,1,0:T(8,128)(2,1)S(1)}, bf16[2,64,512]{2,1,0:T(8,128)(2,1)S(1)}, u32[]{:S(2)}, u32[]{:S(2)}) %collective-permute-start.2) | collective-permute-done | bytes 131104 | tf_op jit(solution)/shard_map/ppermute | solution.py:15
  38.3 0.1 fusion.305
  38.4 0.5 fusion.20
  38.9 0.5 fusion.22
  39.3 0.5 fusion.271
  39.9 0.5 fusion.268
  40.4 2.9 %collective-permute-start.4 = (bf16[2,64,512]{2,1,0:T(8,128)(2,1)S(1)}, bf16[2,64,512]{2,1,0:T(8,128)(2,1)S(1)}, u32[]{:S(2)}, u32[]{:S(2)}) collective-permute-start(bf16[2,64,512]{2,1,0:T(8,128)(2,1)S(1)} %get-tuple-element.13), channel_id=1, source_target_pairs={{0,16},{16,32},{32,48},{48,64},{64,80},{80,96},{96,112},{112,128},... | collective-permute-start | bytes 393224 | tf_op jit(solution)/shard_map/ppermute | solution.py:15
  43.4 1.9 %collective-permute-start.5 = (bf16[2,64,512]{2,1,0:T(8,128)(2,1)S(1)}, bf16[2,64,512]{2,1,0:T(8,128)(2,1)S(1)}, u32[]{:S(2)}, u32[]{:S(2)}) collective-permute-start(bf16[2,64,512]{2,1,0:T(8,128)(2,1)S(1)} %get-tuple-element.14), channel_id=1, source_target_pairs={{0,1},{1,2},{2,3},{3,4},{4,5},{5,6},{6,7},{7,8},{8,9},{9,10},{10,1... | collective-permute-start | bytes 393224 | tf_op jit(solution)/shard_map/ppermute | solution.py:15
  45.3 8.7 %collective-permute-done.4 = bf16[2,64,512]{2,1,0:T(8,128)(2,1)S(1)} collective-permute-done((bf16[2,64,512]{2,1,0:T(8,128)(2,1)S(1)}, bf16[2,64,512]{2,1,0:T(8,128)(2,1)S(1)}, u32[]{:S(2)}, u32[]{:S(2)}) %collective-permute-start.4) | collective-permute-done | bytes 131104 | tf_op jit(solution)/shard_map/ppermute | solution.py:15
  54.0 0.1 fusion.306
  54.0 0.5 fusion.16
  54.5 0.5 fusion.18
  55.0 0.5 fusion.277
  55.5 0.5 fusion.274
  56.1 1.9 %collective-permute-start.6 = (bf16[2,64,512]{2,1,0:T(8,128)(2,1)S(1)}, bf16[2,64,512]{2,1,0:T(8,128)(2,1)S(1)}, u32[]{:S(2)}, u32[]{:S(2)}) collective-permute-start(bf16[2,64,512]{2,1,0:T(8,128)(2,1)S(1)} %get-tuple-element.11), channel_id=1, source_target_pairs={{0,16},{16,32},{32,48},{48,64},{64,80},{80,96},{96,112},{112,128},... | collective-permute-start | bytes 393224 | tf_op jit(solution)/shard_map/ppermute | solution.py:15
  58.0 1.9 %collective-permute-start.7 = (bf16[2,64,512]{2,1,0:T(8,128)(2,1)S(1)}, bf16[2,64,512]{2,1,0:T(8,128)(2,1)S(1)}, u32[]{:S(2)}, u32[]{:S(2)}) collective-permute-start(bf16[2,64,512]{2,1,0:T(8,128)(2,1)S(1)} %get-tuple-element.12), channel_id=1, source_target_pairs={{0,1},{1,2},{2,3},{3,4},{4,5},{5,6},{6,7},{7,8},{8,9},{9,10},{10,1... | collective-permute-start | bytes 393224 | tf_op jit(solution)/shard_map/ppermute | solution.py:15
  60.0 9.0 %collective-permute-done.6 = bf16[2,64,512]{2,1,0:T(8,128)(2,1)S(1)} collective-permute-done((bf16[2,64,512]{2,1,0:T(8,128)(2,1)S(1)}, bf16[2,64,512]{2,1,0:T(8,128)(2,1)S(1)}, u32[]{:S(2)}, u32[]{:S(2)}) %collective-permute-start.6) | collective-permute-done | bytes 131104 | tf_op jit(solution)/shard_map/ppermute | solution.py:15
  69.0 0.1 fusion.307
  69.0 0.5 fusion.12
  69.5 0.5 fusion.14
  70.0 0.5 fusion.283
  70.5 0.5 fusion.280
  71.1 1.9 %collective-permute-start.8 = (bf16[2,64,512]{2,1,0:T(8,128)(2,1)S(1)}, bf16[2,64,512]{2,1,0:T(8,128)(2,1)S(1)}, u32[]{:S(2)}, u32[]{:S(2)}) collective-permute-start(bf16[2,64,512]{2,1,0:T(8,128)(2,1)S(1)} %get-tuple-element.9), channel_id=1, source_target_pairs={{0,16},{16,32},{32,48},{48,64},{64,80},{80,96},{96,112},{112,128},... | collective-permute-start | bytes 393224 | tf_op jit(solution)/shard_map/ppermute | solution.py:15
  73.0 1.9 %collective-permute-start.9 = (bf16[2,64,512]{2,1,0:T(8,128)(2,1)S(1)}, bf16[2,64,512]{2,1,0:T(8,128)(2,1)S(1)}, u32[]{:S(2)}, u32[]{:S(2)}) collective-permute-start(bf16[2,64,512]{2,1,0:T(8,128)(2,1)S(1)} %get-tuple-element.10), channel_id=1, source_target_pairs={{0,1},{1,2},{2,3},{3,4},{4,5},{5,6},{6,7},{7,8},{8,9},{9,10},{10,1... | collective-permute-start | bytes 393224 | tf_op jit(solution)/shard_map/ppermute | solution.py:15
  75.0 8.9 %collective-permute-done.8 = bf16[2,64,512]{2,1,0:T(8,128)(2,1)S(1)} collective-permute-done((bf16[2,64,512]{2,1,0:T(8,128)(2,1)S(1)}, bf16[2,64,512]{2,1,0:T(8,128)(2,1)S(1)}, u32[]{:S(2)}, u32[]{:S(2)}) %collective-permute-start.8) | collective-permute-done | bytes 131104 | tf_op jit(solution)/shard_map/ppermute | solution.py:15
  83.9 0.1 fusion.308
  83.9 0.5 fusion.8
  84.4 0.5 fusion.10
  84.9 0.5 fusion.289
  85.4 0.5 fusion.286
  86.0 1.9 %collective-permute-start.10 = (bf16[2,64,512]{2,1,0:T(8,128)(2,1)S(1)}, bf16[2,64,512]{2,1,0:T(8,128)(2,1)S(1)}, u32[]{:S(2)}, u32[]{:S(2)}) collective-permute-start(bf16[2,64,512]{2,1,0:T(8,128)(2,1)S(1)} %get-tuple-element.7), channel_id=1, source_target_pairs={{0,16},{16,32},{32,48},{48,64},{64,80},{80,96},{96,112},{112,128},... | collective-permute-start | bytes 393224 | tf_op jit(solution)/shard_map/ppermute | solution.py:15
  87.9 1.9 %collective-permute-start.11 = (bf16[2,64,512]{2,1,0:T(8,128)(2,1)S(1)}, bf16[2,64,512]{2,1,0:T(8,128)(2,1)S(1)}, u32[]{:S(2)}, u32[]{:S(2)}) collective-permute-start(bf16[2,64,512]{2,1,0:T(8,128)(2,1)S(1)} %get-tuple-element.8), channel_id=1, source_target_pairs={{0,1},{1,2},{2,3},{3,4},{4,5},{5,6},{6,7},{7,8},{8,9},{9,10},{10,1... | collective-permute-start | bytes 393224 | tf_op jit(solution)/shard_map/ppermute | solution.py:15
  89.9 8.3 %collective-permute-done.10 = bf16[2,64,512]{2,1,0:T(8,128)(2,1)S(1)} collective-permute-done((bf16[2,64,512]{2,1,0:T(8,128)(2,1)S(1)}, bf16[2,64,512]{2,1,0:T(8,128)(2,1)S(1)}, u32[]{:S(2)}, u32[]{:S(2)}) %collective-permute-start.10) | collective-permute-done | bytes 131104 | tf_op jit(solution)/shard_map/ppermute | solution.py:15
  98.2 0.5 fusion.4
  98.7 0.5 fusion.6
  99.2 0.5 fusion.295
  99.7 0.5 fusion.292
  100.3 1.9 %collective-permute-start.12 = (bf16[2,64,512]{2,1,0:T(8,128)(2,1)S(1)}, bf16[2,64,512]{2,1,0:T(8,128)(2,1)S(1)}, u32[]{:S(2)}, u32[]{:S(2)}) collective-permute-start(bf16[2,64,512]{2,1,0:T(8,128)(2,1)S(1)} %get-tuple-element.5), channel_id=1, source_target_pairs={{0,16},{16,32},{32,48},{48,64},{64,80},{80,96},{96,112},{112,128},... | collective-permute-start | bytes 393224 | tf_op jit(solution)/shard_map/ppermute | solution.py:15
  102.2 1.9 %collective-permute-start.13 = (bf16[2,64,512]{2,1,0:T(8,128)(2,1)S(1)}, bf16[2,64,512]{2,1,0:T(8,128)(2,1)S(1)}, u32[]{:S(2)}, u32[]{:S(2)}) collective-permute-start(bf16[2,64,512]{2,1,0:T(8,128)(2,1)S(1)} %get-tuple-element.6), channel_id=1, source_target_pairs={{0,1},{1,2},{2,3},{3,4},{4,5},{5,6},{6,7},{7,8},{8,9},{9,10},{10,1... | collective-permute-start | bytes 393224 | tf_op jit(solution)/shard_map/ppermute | solution.py:15
  104.1 8.3 %collective-permute-done.12 = bf16[2,64,512]{2,1,0:T(8,128)(2,1)S(1)} collective-permute-done((bf16[2,64,512]{2,1,0:T(8,128)(2,1)S(1)}, bf16[2,64,512]{2,1,0:T(8,128)(2,1)S(1)}, u32[]{:S(2)}, u32[]{:S(2)}) %collective-permute-start.12) | collective-permute-done | bytes 131104 | tf_op jit(solution)/shard_map/ppermute | solution.py:15
  112.4 0.1 fusion.310
  112.5 0.5 fusion
  113.0 0.5 fusion.2
  113.5 0.5 fusion.301
  114.0 0.5 fusion.298
  114.6 0.7 pad_maximum_fusion
  (22 shorter events, 0.3 us)
Async XLA Ops:
  0.0 4.7 %copy-start = (bf16[1,1,2,64,1024]{4,3,2,1,0:T(8,128)(2,1)S(1)}, bf16[1,1,2,64,1024]{4,3,2,1,0:T(8,128)(2,1)}, u32[]{:S(2)}) copy-start(bf16[1,1,2,64,1024]{4,3,2,1,0:T(8,128)(2,1)} %param.4) | copy-start | bytes 786436
  0.0 4.4 %copy-start.2 = (s32[8]{0:T(128)S(1)}, s32[8]{0:T(128)}, u32[]{:S(2)}) copy-start(s32[8]{0:T(128)} %param.5) | copy-start | bytes 100
  4.7 18.6 %copy-start.1 = (bf16[1,1,2,1024,1024]{4,3,2,1,0:T(8,128)(2,1)S(1)}, bf16[1,1,2,1024,1024]{4,3,2,1,0:T(8,128)(2,1)}, u32[]{:S(2)}) copy-start(bf16[1,1,2,1024,1024]{4,3,2,1,0:T(8,128)(2,1)} %param.3) | copy-start | bytes 12582916
  9.2 14.0 %collective-permute-start = (bf16[2,64,512]{2,1,0:T(8,128)(2,1)S(1)}, bf16[2,64,512]{2,1,0:T(8,128)(2,1)S(1)}, u32[]{:S(2)}, u32[]{:S(2)}) collective-permute-start(bf16[2,64,512]{2,1,0:T(8,128)(2,1)S(1)} %get-tuple-element.17), channel_id=1, source_target_pairs={{0,16},{16,32},{32,48},{48,64},{64,80},{80,96},{96,112},{112,128},... | collective-permute-start | bytes 393224 | tf_op jit(solution)/shard_map/ppermute | solution.py:15
  13.7 9.5 %collective-permute-start.1 = (bf16[2,64,512]{2,1,0:T(8,128)(2,1)S(1)}, bf16[2,64,512]{2,1,0:T(8,128)(2,1)S(1)}, u32[]{:S(2)}, u32[]{:S(2)}) collective-permute-start(bf16[2,64,512]{2,1,0:T(8,128)(2,1)S(1)} %get-tuple-element.18), channel_id=1, source_target_pairs={{0,1},{1,2},{2,3},{3,4},{4,5},{5,6},{6,7},{7,8},{8,9},{9,10},{10,1... | collective-permute-start | bytes 393224 | tf_op jit(solution)/shard_map/ppermute | solution.py:15
  25.4 12.9 %collective-permute-start.2 = (bf16[2,64,512]{2,1,0:T(8,128)(2,1)S(1)}, bf16[2,64,512]{2,1,0:T(8,128)(2,1)S(1)}, u32[]{:S(2)}, u32[]{:S(2)}) collective-permute-start(bf16[2,64,512]{2,1,0:T(8,128)(2,1)S(1)} %get-tuple-element.15), channel_id=1, source_target_pairs={{0,16},{16,32},{32,48},{48,64},{64,80},{80,96},{96,112},{112,128},... | collective-permute-start | bytes 393224 | tf_op jit(solution)/shard_map/ppermute | solution.py:15
  29.3 9.0 %collective-permute-start.3 = (bf16[2,64,512]{2,1,0:T(8,128)(2,1)S(1)}, bf16[2,64,512]{2,1,0:T(8,128)(2,1)S(1)}, u32[]{:S(2)}, u32[]{:S(2)}) collective-permute-start(bf16[2,64,512]{2,1,0:T(8,128)(2,1)S(1)} %get-tuple-element.16), channel_id=1, source_target_pairs={{0,1},{1,2},{2,3},{3,4},{4,5},{5,6},{6,7},{7,8},{8,9},{9,10},{10,1... | collective-permute-start | bytes 393224 | tf_op jit(solution)/shard_map/ppermute | solution.py:15
  40.4 13.5 %collective-permute-start.4 = (bf16[2,64,512]{2,1,0:T(8,128)(2,1)S(1)}, bf16[2,64,512]{2,1,0:T(8,128)(2,1)S(1)}, u32[]{:S(2)}, u32[]{:S(2)}) collective-permute-start(bf16[2,64,512]{2,1,0:T(8,128)(2,1)S(1)} %get-tuple-element.13), channel_id=1, source_target_pairs={{0,16},{16,32},{32,48},{48,64},{64,80},{80,96},{96,112},{112,128},... | collective-permute-start | bytes 393224 | tf_op jit(solution)/shard_map/ppermute | solution.py:15
  43.4 10.6 %collective-permute-start.5 = (bf16[2,64,512]{2,1,0:T(8,128)(2,1)S(1)}, bf16[2,64,512]{2,1,0:T(8,128)(2,1)S(1)}, u32[]{:S(2)}, u32[]{:S(2)}) collective-permute-start(bf16[2,64,512]{2,1,0:T(8,128)(2,1)S(1)} %get-tuple-element.14), channel_id=1, source_target_pairs={{0,1},{1,2},{2,3},{3,4},{4,5},{5,6},{6,7},{7,8},{8,9},{9,10},{10,1... | collective-permute-start | bytes 393224 | tf_op jit(solution)/shard_map/ppermute | solution.py:15
  56.1 12.9 %collective-permute-start.6 = (bf16[2,64,512]{2,1,0:T(8,128)(2,1)S(1)}, bf16[2,64,512]{2,1,0:T(8,128)(2,1)S(1)}, u32[]{:S(2)}, u32[]{:S(2)}) collective-permute-start(bf16[2,64,512]{2,1,0:T(8,128)(2,1)S(1)} %get-tuple-element.11), channel_id=1, source_target_pairs={{0,16},{16,32},{32,48},{48,64},{64,80},{80,96},{96,112},{112,128},... | collective-permute-start | bytes 393224 | tf_op jit(solution)/shard_map/ppermute | solution.py:15
  58.0 10.9 %collective-permute-start.7 = (bf16[2,64,512]{2,1,0:T(8,128)(2,1)S(1)}, bf16[2,64,512]{2,1,0:T(8,128)(2,1)S(1)}, u32[]{:S(2)}, u32[]{:S(2)}) collective-permute-start(bf16[2,64,512]{2,1,0:T(8,128)(2,1)S(1)} %get-tuple-element.12), channel_id=1, source_target_pairs={{0,1},{1,2},{2,3},{3,4},{4,5},{5,6},{6,7},{7,8},{8,9},{9,10},{10,1... | collective-permute-start | bytes 393224 | tf_op jit(solution)/shard_map/ppermute | solution.py:15
  71.1 12.7 %collective-permute-start.8 = (bf16[2,64,512]{2,1,0:T(8,128)(2,1)S(1)}, bf16[2,64,512]{2,1,0:T(8,128)(2,1)S(1)}, u32[]{:S(2)}, u32[]{:S(2)}) collective-permute-start(bf16[2,64,512]{2,1,0:T(8,128)(2,1)S(1)} %get-tuple-element.9), channel_id=1, source_target_pairs={{0,16},{16,32},{32,48},{48,64},{64,80},{80,96},{96,112},{112,128},... | collective-permute-start | bytes 393224 | tf_op jit(solution)/shard_map/ppermute | solution.py:15
  73.0 10.8 %collective-permute-start.9 = (bf16[2,64,512]{2,1,0:T(8,128)(2,1)S(1)}, bf16[2,64,512]{2,1,0:T(8,128)(2,1)S(1)}, u32[]{:S(2)}, u32[]{:S(2)}) collective-permute-start(bf16[2,64,512]{2,1,0:T(8,128)(2,1)S(1)} %get-tuple-element.10), channel_id=1, source_target_pairs={{0,1},{1,2},{2,3},{3,4},{4,5},{5,6},{6,7},{7,8},{8,9},{9,10},{10,1... | collective-permute-start | bytes 393224 | tf_op jit(solution)/shard_map/ppermute | solution.py:15
  86.0 12.1 %collective-permute-start.10 = (bf16[2,64,512]{2,1,0:T(8,128)(2,1)S(1)}, bf16[2,64,512]{2,1,0:T(8,128)(2,1)S(1)}, u32[]{:S(2)}, u32[]{:S(2)}) collective-permute-start(bf16[2,64,512]{2,1,0:T(8,128)(2,1)S(1)} %get-tuple-element.7), channel_id=1, source_target_pairs={{0,16},{16,32},{32,48},{48,64},{64,80},{80,96},{96,112},{112,128},... | collective-permute-start | bytes 393224 | tf_op jit(solution)/shard_map/ppermute | solution.py:15
  87.9 10.2 %collective-permute-start.11 = (bf16[2,64,512]{2,1,0:T(8,128)(2,1)S(1)}, bf16[2,64,512]{2,1,0:T(8,128)(2,1)S(1)}, u32[]{:S(2)}, u32[]{:S(2)}) collective-permute-start(bf16[2,64,512]{2,1,0:T(8,128)(2,1)S(1)} %get-tuple-element.8), channel_id=1, source_target_pairs={{0,1},{1,2},{2,3},{3,4},{4,5},{5,6},{6,7},{7,8},{8,9},{9,10},{10,1... | collective-permute-start | bytes 393224 | tf_op jit(solution)/shard_map/ppermute | solution.py:15
  100.3 12.2 %collective-permute-start.12 = (bf16[2,64,512]{2,1,0:T(8,128)(2,1)S(1)}, bf16[2,64,512]{2,1,0:T(8,128)(2,1)S(1)}, u32[]{:S(2)}, u32[]{:S(2)}) collective-permute-start(bf16[2,64,512]{2,1,0:T(8,128)(2,1)S(1)} %get-tuple-element.5), channel_id=1, source_target_pairs={{0,16},{16,32},{32,48},{48,64},{64,80},{80,96},{96,112},{112,128},... | collective-permute-start | bytes 393224 | tf_op jit(solution)/shard_map/ppermute | solution.py:15
  102.2 10.2 %collective-permute-start.13 = (bf16[2,64,512]{2,1,0:T(8,128)(2,1)S(1)}, bf16[2,64,512]{2,1,0:T(8,128)(2,1)S(1)}, u32[]{:S(2)}, u32[]{:S(2)}) collective-permute-start(bf16[2,64,512]{2,1,0:T(8,128)(2,1)S(1)} %get-tuple-element.6), channel_id=1, source_target_pairs={{0,1},{1,2},{2,3},{3,4},{4,5},{5,6},{6,7},{7,8},{8,9},{9,10},{10,1... | collective-permute-start | bytes 393224 | tf_op jit(solution)/shard_map/ppermute | solution.py:15
where the time goes:
time: 116 us; the launch traced here: 115 us
  waiting for transfers between devices  57.8 us (50%)
  starting transfers between devices  32.5 us (28%)
  matrix products  22.9 us (20%)
  other arithmetic  1.37 us (1%)
    ppermute x14, waiting for transfers between devices, shifted(): return lax.ppermute(block, axis, route)  57.8 us
    ppermute x14, starting transfers between devices, shifted(): return lax.ppermute(block, axis, route)  32.5 us
    dot_general x8, matrix products, apply_block(): jnp.dot(u_im, w_re, preferred_element_type=jnp.float32)  5.99 us
    dot_general x8, matrix products, apply_block(): jnp.dot(u_re, w_re, preferred_element_type=jnp.float32)  5.87 us
    dot_general x8, matrix products, apply_block(): jnp.dot(u_re, w_im, preferred_element_type=jnp.float32)  5.53 us
    dot_general x8, matrix products, apply_block(): jnp.dot(u_im, w_im, preferred_element_type=jnp.float32)  5.48 us
  transfers between devices with their start and end apart: 14, of which 7 were waited for; matrix products, arithmetic and copies ran while one was open for 0% of the time, Pallas kernels for 0%

commit v1 on v0

v1 whole, which is shorter than its diff:
```python
import functools
import math

import jax
import jax.numpy as jnp
from jax import lax
from jax.experimental import pallas as pl
from jax.experimental.pallas import tpu as pltpu
from jax.sharding import PartitionSpec as P

SPANS = 8
SECTIONS = 8
CHUNKS = 2
PIECES = 4
MESH = pl.DeviceIdType.MESH


def kernel(
    n_gx, n_gy, nodes_ref, w_hbm, src_hbm, out_hbm,
    w, src, in_left, in_bottom, out_right, out_top, sig_re, sig_im,
    w_sem, src_sem, out_sem, send_right, recv_left, send_top, recv_bottom,
):
    gx, gy = lax.axis_index("gx"), lax.axis_index("gy")
    rows, order = src.shape[1], src.shape[2]
    edge = order // 2
    step = rows // CHUNKS
    depth = order // PIECES
    has_left, has_bottom = gx > 0, gy > 0
    has_right, has_top = gx < n_gx - 1, gy < n_gy - 1

    load_src = pltpu.make_async_copy(src_hbm, src, src_sem)
    load_src.start()

    def load_w(half, piece):
        part = (slice(None), pl.ds(piece * depth, depth), pl.ds(half * edge, edge))
        return pltpu.make_async_copy(w_hbm.at[part], w.at[part], w_sem.at[half, piece])

    for half in range(2):
        for piece in range(PIECES):
            load_w(half, piece).start()

    barrier = pltpu.get_barrier_semaphore()
    neighbours = (
        (has_left, (gx - 1, gy)), (has_right, (gx + 1, gy)),
        (has_bottom, (gx, gy - 1)), (has_top, (gx, gy + 1)),
    )
    for there, device in neighbours:
        @pl.when(there)
        def _():
            pl.semaphore_signal(barrier, inc=1, device_id=device, device_id_type=MESH)

    @pl.when(jnp.logical_not(has_left))
    def _():
        in_left[...] = jnp.zeros_like(in_left)

    @pl.when(jnp.logical_not(has_bottom))
    def _():
        in_bottom[...] = jnp.zeros_like(in_bottom)

    block = rows // SPANS
    nodes = jnp.concatenate(
        [jnp.full((block, 128), nodes_ref[b].astype(jnp.float32)) for b in range(SPANS)], axis=0
    )
    angles = math.pi * (nodes + 0.5) / SPANS
    sig_re[...] = 0.5 * jnp.cos(angles)
    sig_im[...] = 0.5 * jnp.sin(angles)

    def send(side, section, chunk):
        if side == 0:
            return pltpu.make_async_remote_copy(
                src_ref=out_right.at[section, chunk], dst_ref=in_left.at[section, chunk],
                send_sem=send_right.at[section, chunk], recv_sem=recv_left.at[section, chunk],
                device_id=(gx + 1, gy), device_id_type=MESH,
            )
        return pltpu.make_async_remote_copy(
            src_ref=out_top.at[section, chunk], dst_ref=in_bottom.at[section, chunk],
            send_sem=send_top.at[section, chunk], recv_sem=recv_bottom.at[section, chunk],
            device_id=(gx, gy + 1), device_id_type=MESH,
        )

    def finish(side, section, chunk, driven, real, imag):
        span = pl.ds(chunk * step, step)
        f = driven[:, side * edge:(side + 1) * edge].astype(jnp.float32)
        f_re, f_im = f[:step], f[step:]
        s_re = jnp.concatenate([sig_re[span, :]] * (edge // 128), axis=1)
        s_im = jnp.concatenate([sig_im[span, :]] * (edge // 128), axis=1)
        out = out_right if side == 0 else out_top
        out[section, chunk, 0] = (real + s_re * f_re - s_im * f_im).astype(jnp.bfloat16)
        out[section, chunk, 1] = (imag + s_re * f_im + s_im * f_re).astype(jnp.bfloat16)

    def product(driven, side, first, size):
        u = driven[:, first:first + size]
        columns = slice(side * edge, (side + 1) * edge)
        p = jnp.dot(u, w[0, first:first + size, columns], preferred_element_type=jnp.float32)
        q = jnp.dot(u, w[1, first:first + size, columns], preferred_element_type=jnp.float32)
        return p[:step] - q[step:], q[:step] + p[step:]

    def source(chunk):
        span = pl.ds(chunk * step, step)
        return jnp.concatenate([src[0, span, :], src[1, span, :]], axis=0)

    load_src.wait()
    for side in range(2):
        totals = [[0.0, 0.0] for _ in range(CHUNKS)]
        for piece in range(PIECES):
            load_w(side, piece).wait()
            for chunk in range(CHUNKS):
                real, imag = product(source(chunk), side, piece * depth, depth)
                totals[chunk][0] += real
                totals[chunk][1] += imag
        for chunk in range(CHUNKS):
            finish(side, 0, chunk, source(chunk), *totals[chunk])
            if side == 0 and chunk == 0:
                pl.semaphore_wait(
                    barrier,
                    has_left.astype(jnp.int32) + has_right.astype(jnp.int32)
                    + has_bottom.astype(jnp.int32) + has_top.astype(jnp.int32),
                )

            @pl.when(has_right if side == 0 else has_top)
            def _():
                send(side, 0, chunk).start()

    def section_body(section, _):
        for chunk in range(CHUNKS):
            @pl.when(has_bottom)
            def _():
                send(1, section - 1, chunk).wait_recv()

            @pl.when(has_left)
            def _():
                send(0, section - 1, chunk).wait_recv()

            span = pl.ds(chunk * step, step)
            driven = jnp.concatenate(
                [
                    jnp.concatenate(
                        [
                            in_left[section - 1, chunk, part].astype(jnp.float32),
                            in_bottom[section - 1, chunk, part].astype(jnp.float32),
                        ],
                        axis=1,
                    )
                    + src[part, span, :].astype(jnp.float32)
                    for part in range(2)
                ],
                axis=0,
            ).astype(jnp.bfloat16)
            for side in range(2):
                real, imag = product(driven, side, 0, order)
                finish(side, section, chunk, driven, real, imag)

                @pl.when(jnp.logical_and(has_right if side == 0 else has_top, section < SECTIONS - 1))
                def _():
                    send(side, section, chunk).start()
        return 0

    lax.fori_loop(1, SECTIONS, section_body, 0)

    def store(side, chunk):
        out = out_right if side == 0 else out_top
        return pltpu.make_async_copy(
            out.at[SECTIONS - 1, chunk],
            out_hbm.at[:, pl.ds(chunk * step, step), pl.ds(side * edge, edge)],
            out_sem.at[side, chunk],
        )

    for chunk in range(CHUNKS):
        for side in range(2):
            store(side, chunk).start()

    def drain(section, _):
        for chunk in range(CHUNKS):
            @pl.when(has_right)
            def _():
                send(0, section, chunk).wait_send()

            @pl.when(has_top)
            def _():
                send(1, section, chunk).wait_send()
        return 0

    lax.fori_loop(0, SECTIONS - 1, drain, 0)
    for chunk in range(CHUNKS):
        for side in range(2):
            store(side, chunk).wait()


def solution(mesh):
    n_gx, n_gy = mesh.shape["gx"], mesh.shape["gy"]

    def per_device(transfer, sources, quad_nodes):
        weights, source = transfer[0, 0], sources[0, 0]
        _, rows, order = source.shape
        step, edge = rows // CHUNKS, order // 2
        moved = SECTIONS - 1
        dma = pltpu.SemaphoreType.DMA
        outgoing = pl.pallas_call(
            functools.partial(kernel, n_gx, n_gy),
            out_shape=jax.ShapeDtypeStruct(source.shape, jnp.bfloat16),
            in_specs=[
                pl.BlockSpec(memory_space=pltpu.SMEM),
                pl.BlockSpec(memory_space=pl.ANY),
                pl.BlockSpec(memory_space=pl.ANY),
            ],
            out_specs=pl.BlockSpec(memory_space=pl.ANY),
            scratch_shapes=[
                pltpu.VMEM(weights.shape, jnp.bfloat16),
                pltpu.VMEM(source.shape, jnp.bfloat16),
                pltpu.VMEM((moved, CHUNKS, 2, step, edge), jnp.bfloat16),
                pltpu.VMEM((moved, CHUNKS, 2, step, edge), jnp.bfloat16),
                pltpu.VMEM((SECTIONS, CHUNKS, 2, step, edge), jnp.bfloat16),
                pltpu.VMEM((SECTIONS, CHUNKS, 2, step, edge), jnp.bfloat16),
                pltpu.VMEM((rows, 128), jnp.float32),
                pltpu.VMEM((rows, 128), jnp.float32),
                dma((2, PIECES)),
                dma,
                dma((2, CHUNKS)),
                dma((moved, CHUNKS)),
                dma((moved, CHUNKS)),
                dma((moved, CHUNKS)),
                dma((moved, CHUNKS)),
            ],
            compiler_params=pltpu.CompilerParams(
                collective_id=0, has_side_effects=True, vmem_limit_bytes=60 * 1024 * 1024
            ),
        )(quad_nodes, weights, source)
        return outgoing[None, None]

    return jax.shard_map(
        per_device,
        mesh=mesh,
        in_specs=(P("gx", "gy", None, None, None), P("gx", "gy", None, None, None), P()),
        out_specs=P("gx", "gy", None, None, None),
        check_vma=False,
    )
```

time: 116 us -> 64.1 us (0.55)
  the two profiles are of different devices: /device:TPU:264 before, /device:TPU:76 now
where the time goes in v1:
time: 64.1 us; the launch traced here: 63.9 us
  Pallas kernels  62.2 us (97%)
  local copies, waits for them, and re-layouts  1.67 us (3%)
    pallas_call x1, Pallas kernels, per_device(): pl.pallas_call(functools.partial(kernel, n_gx, n_gy), out_shape=jax.Shape...  62.2 us
    unnamed x1, local copies, waits for them, and re-layouts  1.67 us

profile of v1, /device:TPU:76, one launch (start us, length us, event | category | flops | bytes accessed | tf_op | source)
XLA Modules:
  0.0 63.9 jit_solution(13968500819686538229)
XLA Ops:
  0.0 62.2 %shard_map.37 = bf16[2,64,1024]{2,1,0:T(8,128)(2,1)} custom-call(s32[8]{0:T(128)} %nodes_ref.1, bf16[2,1024,1024]{2,1,0:T(8,128)(2,1)} %bitcast.3, bf16[2,64,1024]{2,1,0:T(8,128)(2,1)} %bitcast.5), custom_call_target="tpu_custom_call" | custom-call | tf_op jit(solution)/shard_map/pallas_call | solution.py:198
  62.3 1.7 %copy.5 = bf16[1,1,2,64,1024]{4,3,2,1,0:T(8,128)(2,1)} copy(bf16[1,1,2,64,1024]{4,3,2,1,0:T(8,128)(2,1)} %bitcast.4) | data formatting | bytes 524288

commit v2 on v1

v2 whole, which is shorter than its diff:
```python
import functools
import math

import jax
import jax.numpy as jnp
from jax import lax
from jax.experimental import pallas as pl
from jax.experimental.pallas import tpu as pltpu
from jax.sharding import PartitionSpec as P

SPANS = 8
SECTIONS = 8
GROUPS = 4
PIECES = 4
PERIOD = 2
RELAY_SLOT = (4, 0)
FIRST_SLOT = (0, 2)
Y_HI, Y_LO, CORES = 4, 2, 2
RING = Y_HI * Y_LO
BACK = 3
MESH = pl.DeviceIdType.MESH


def kernel(
    n_gx, n_gy, nodes_ref, w_hbm, src_hbm, out_hbm,
    w, src, in_left, in_bottom, out_right, out_top, relay, sig_re, sig_im,
    w_sem, src_sem, out_sem, send_right, recv_left, send_top, recv_bottom, recv_relay, send_relay,
):
    gx, gy = lax.axis_index("gx"), lax.axis_index("gy")
    step, order = src.shape[2], src.shape[3]
    edge = order // 2
    depth = order // PIECES
    has_left, has_bottom = gx > 0, gy > 0
    has_right, has_top = gx < n_gx - 1, gy < n_gy - 1

    z, y = gx // Y_HI, (gx % Y_HI) * Y_LO + (gy // CORES) % Y_LO

    def on_ring(level, place):
        column = level * Y_HI + place // Y_LO
        row = (gy // (Y_LO * CORES)) * (Y_LO * CORES) + (place % Y_LO) * CORES + gy % CORES
        return column, row

    behind, ahead = (y + RING - BACK) % RING, (y + BACK) % RING
    relay_to = on_ring(z, behind)
    relay_from = on_ring(z, ahead)
    has_relay = relay_from[0] < n_gx - 1
    last_to = on_ring(z + (ahead // Y_LO + 1) // Y_HI, behind)
    origin = gx - 1
    last_from = on_ring(origin // Y_HI, ((origin % Y_HI) * Y_LO + (gy // CORES) % Y_LO + RING - BACK) % RING)

    def load_src(group):
        return pltpu.make_async_copy(
            src_hbm.at[:, pl.ds(group * step, step), :], src.at[group], src_sem.at[group]
        )

    def load_w(half, piece):
        part = (slice(None), pl.ds(piece * depth, depth), pl.ds(half * edge, edge))
        return pltpu.make_async_copy(w_hbm.at[part], w.at[part], w_sem.at[half, piece])

    barrier = pltpu.get_barrier_semaphore()
    for there, device in (
        (has_left, (gx - 1, gy)), (has_bottom, (gx, gy - 1)),
        (has_relay, relay_from), (has_left, last_from),
    ):
        @pl.when(there)
        def _():
            pl.semaphore_signal(barrier, inc=1, device_id=device, device_id_type=MESH)

    for group in range(GROUPS):
        load_src(group).start()
    for half in range(2):
        for piece in range(PIECES):
            load_w(half, piece).start()

    @pl.when(jnp.logical_not(has_left))
    def _():
        in_left[...] = jnp.zeros_like(in_left)

    @pl.when(jnp.logical_not(has_bottom))
    def _():
        in_bottom[...] = jnp.zeros_like(in_bottom)

    block = GROUPS * step // SPANS
    nodes = jnp.concatenate(
        [jnp.full((block, 128), nodes_ref[b].astype(jnp.float32)) for b in range(SPANS)], axis=0
    )
    angles = math.pi * (nodes + 0.5) / SPANS
    sig_re[...] = (0.5 * jnp.cos(angles)).reshape(sig_re.shape)
    sig_im[...] = (0.5 * jnp.sin(angles)).reshape(sig_im.shape)

    def copy_out(out, section, group, dst, send_sem, recv_sem, device):
        return pltpu.make_async_remote_copy(
            src_ref=out.at[section, group], dst_ref=dst,
            send_sem=send_sem.at[section, group], recv_sem=recv_sem,
            device_id=device, device_id_type=MESH,
        )

    def direct(section, group):
        return copy_out(
            out_right, section, group, in_left.at[section, group],
            send_right, recv_left.at[section, group], (gx + 1, gy),
        )

    def first_leg(section, group):
        return copy_out(
            out_right, section, group, relay.at[section],
            send_right, recv_relay.at[section], relay_to,
        )

    def last_leg(section, group):
        return pltpu.make_async_remote_copy(
            src_ref=relay.at[section], dst_ref=in_left.at[section, group],
            send_sem=send_relay.at[section], recv_sem=recv_left.at[section, group],
            device_id=last_to, device_id_type=MESH,
        )

    def upward(section, group):
        return copy_out(
            out_top, section, group, in_bottom.at[section, group],
            send_top, recv_bottom.at[section, group], (gx, gy + 1),
        )

    def turned(section):
        return section % PERIOD == 0

    def first_group(section):
        return (section + PERIOD - 1) // PERIOD % GROUPS

    def send(side, place, section, group):
        if side == 1:
            upward(section, group).start()
        elif place > 0:
            direct(section, group).start()
        else:
            @pl.when(turned(section))
            def _():
                first_leg(section, group).start()

            @pl.when(jnp.logical_not(turned(section)))
            def _():
                direct(section, group).start()

    def pass_on(section, when):
        @pl.when(jnp.logical_and(has_relay, jnp.logical_and(when, turned(section))))
        def _():
            first_leg(section, 0).wait_recv()
            last_leg(section, first_group(section)).start()

    def product(u, side, first, size):
        half = u.shape[0] // 2
        columns = slice(side * edge, (side + 1) * edge)
        p = jnp.dot(u, w[0, first:first + size, columns], preferred_element_type=jnp.float32)
        q = jnp.dot(u, w[1, first:first + size, columns], preferred_element_type=jnp.float32)
        return p[:half] - q[half:], q[:half] + p[half:]

    def finish(side, section, group, f_re, f_im, real, imag):
        s_re = jnp.concatenate([sig_re[group]] * (edge // 128), axis=1)
        s_im = jnp.concatenate([sig_im[group]] * (edge // 128), axis=1)
        out = out_right if side == 0 else out_top
        out[section, group, 0] = (real + s_re * f_re - s_im * f_im).astype(jnp.bfloat16)
        out[section, group, 1] = (imag + s_re * f_im + s_im * f_re).astype(jnp.bfloat16)

    for group in range(GROUPS):
        load_src(group).wait()
    for side in range(2):
        real, imag = 0.0, 0.0
        columns = slice(side * edge, (side + 1) * edge)
        for piece in range(PIECES):
            load_w(side, piece).wait()
            part = slice(piece * depth, (piece + 1) * depth)
            u = jnp.concatenate(
                [src[group, c, :, part] for c in range(2) for group in range(GROUPS)], axis=0
            )
            more_real, more_imag = product(u, side, 0 + piece * depth, depth)
            real += more_real
            imag += more_imag
        for group in range(GROUPS):
            rows = slice(group * step, (group + 1) * step)
            finish(
                side, 0, group,
                src[group, 0, :, columns].astype(jnp.float32),
                src[group, 1, :, columns].astype(jnp.float32),
                real[rows], imag[rows],
            )
        if side == 0:
            pl.semaphore_wait(
                barrier, 2 * has_right.astype(jnp.int32) + has_top.astype(jnp.int32) + has_relay.astype(jnp.int32)
            )
        for group in range(GROUPS):
            @pl.when(has_right if side == 0 else has_top)
            def _():
                send(side, group, jnp.int32(0), group)

    def section_body(section, _):
        more = section < SECTIONS - 1

        def relay_slot(place, phase):
            if (place, phase) == FIRST_SLOT:
                pass_on(section - 1, section == 1)
            if (place, phase) == RELAY_SLOT:
                pass_on(section, more)
            if (place + GROUPS, phase) == RELAY_SLOT and place + phase > 0:
                pass_on(section - 1, section > 1)

        for place in range(GROUPS):
            group = (first_group(section) + place) % GROUPS
            relay_slot(place, 0)

            def arrived(buffer, columns):
                return [
                    (
                        buffer[section - 1, group, part].astype(jnp.float32)
                        + src[group, part, :, columns].astype(jnp.float32)
                    ).astype(jnp.bfloat16)
                    for part in range(2)
                ]

            @pl.when(has_bottom)
            def _():
                upward(section - 1, group).wait_recv()

            lower = arrived(in_bottom, slice(edge, order))
            u = jnp.concatenate(lower, axis=0)
            partial = [product(u, side, edge, edge) for side in range(2)]
            relay_slot(place, 1)

            @pl.when(has_left)
            def _():
                direct(section - 1, group).wait_recv()

            upper = arrived(in_left, slice(0, edge))
            u = jnp.concatenate(upper, axis=0)
            for side, driven in ((0, upper), (1, lower)):
                real, imag = product(u, side, 0, edge)
                finish(
                    side, section, group,
                    driven[0].astype(jnp.float32), driven[1].astype(jnp.float32),
                    partial[side][0] + real, partial[side][1] + imag,
                )

                @pl.when(jnp.logical_and(has_right if side == 0 else has_top, more))
                def _():
                    send(side, place, section, group)

                if side == 0:
                    relay_slot(place, 2)
        relay_slot(GROUPS, 0)
        return 0

    lax.fori_loop(1, SECTIONS, section_body, 0)

    def store(side, group):
        out = out_right if side == 0 else out_top
        return pltpu.make_async_copy(
            out.at[SECTIONS - 1, group],
            out_hbm.at[:, pl.ds(group * step, step), pl.ds(side * edge, edge)],
            out_sem.at[side, group],
        )

    for group in range(GROUPS):
        for side in range(2):
            store(side, group).start()

    def drain(section, _):
        for group in range(GROUPS):
            @pl.when(has_right)
            def _():
                direct(section, group).wait_send()

            @pl.when(has_top)
            def _():
                upward(section, group).wait_send()

        @pl.when(jnp.logical_and(has_relay, turned(section)))
        def _():
            last_leg(section, 0).wait_send()
        return 0

    lax.fori_loop(0, SECTIONS - 1, drain, 0)
    for group in range(GROUPS):
        for side in range(2):
            store(side, group).wait()


def solution(mesh):
    n_gx, n_gy = mesh.shape["gx"], mesh.shape["gy"]

    def per_device(transfer, sources, quad_nodes):
        weights, source = transfer[0, 0], sources[0, 0]
        _, rows, order = source.shape
        step, edge = rows // GROUPS, order // 2
        moved = SECTIONS - 1
        dma = pltpu.SemaphoreType.DMA
        vmem = pltpu.VMEM
        outgoing = pl.pallas_call(
            functools.partial(kernel, n_gx, n_gy),
            out_shape=jax.ShapeDtypeStruct(source.shape, jnp.bfloat16),
            in_specs=[
                pl.BlockSpec(memory_space=pltpu.SMEM),
                pl.BlockSpec(memory_space=pl.ANY),
                pl.BlockSpec(memory_space=pl.ANY),
            ],
            out_specs=pl.BlockSpec(memory_space=pl.ANY),
            scratch_shapes=[
                vmem(weights.shape, jnp.bfloat16),
                vmem((GROUPS, 2, step, order), jnp.bfloat16),
                vmem((moved, GROUPS, 2, step, edge), jnp.bfloat16),
                vmem((moved, GROUPS, 2, step, edge), jnp.bfloat16),
                vmem((SECTIONS, GROUPS, 2, step, edge), jnp.bfloat16),
                vmem((SECTIONS, GROUPS, 2, step, edge), jnp.bfloat16),
                vmem((moved, 2, step, edge), jnp.bfloat16),
                vmem((GROUPS, step, 128), jnp.float32),
                vmem((GROUPS, step, 128), jnp.float32),
                dma((2, PIECES)),
                dma((GROUPS,)),
                dma((2, GROUPS)),
                dma((moved, GROUPS)),
                dma((moved, GROUPS)),
                dma((moved, GROUPS)),
                dma((moved, GROUPS)),
                dma((moved,)),
                dma((moved,)),
            ],
            compiler_params=pltpu.CompilerParams(
                collective_id=0, has_side_effects=True, vmem_limit_bytes=60 * 1024 * 1024
            ),
        )(quad_nodes, weights, source)
        return outgoing[None, None]

    return jax.shard_map(
        per_device,
        mesh=mesh,
        in_specs=(P("gx", "gy", None, None, None), P("gx", "gy", None, None, None), P()),
        out_specs=P("gx", "gy", None, None, None),
        check_vma=False,
    )
```

time: 64.1 us -> 58.1 us (0.906)
  the two profiles are of different devices: /device:TPU:76 before, /device:TPU:212 now
where the time goes in v2:
time: 58.1 us; the launch traced here: 58 us
  Pallas kernels  56.3 us (97%)
  local copies, waits for them, and re-layouts  1.67 us (3%)
    pallas_call x1, Pallas kernels, per_device(): pl.pallas_call(functools.partial(kernel, n_gx, n_gy), out_shape=jax.Shape...  56.3 us
    unnamed x1, local copies, waits for them, and re-layouts  1.67 us

profile of v2, /device:TPU:212, one launch (start us, length us, event | category | flops | bytes accessed | tf_op | source)
XLA Modules:
  0.0 58.0 jit_solution(774828194095905029)
XLA Ops:
  0.0 56.3 %shard_map.37 = bf16[2,64,1024]{2,1,0:T(8,128)(2,1)} custom-call(s32[8]{0:T(128)} %nodes_ref.1, bf16[2,1024,1024]{2,1,0:T(8,128)(2,1)} %bitcast.3, bf16[2,64,1024]{2,1,0:T(8,128)(2,1)} %bitcast.5), custom_call_target="tpu_custom_call" | custom-call | tf_op jit(solution)/shard_map/pallas_call | solution.py:295
  56.3 1.7 %copy.5 = bf16[1,1,2,64,1024]{4,3,2,1,0:T(8,128)(2,1)} copy(bf16[1,1,2,64,1024]{4,3,2,1,0:T(8,128)(2,1)} %bitcast.4) | data formatting | bytes 524288

commit v3 on v2

--- a/solution.py
+++ b/solution.py
@@ -22,9 +22,9 @@
 
 
 def kernel(
-    n_gx, n_gy, nodes_ref, w_hbm, src_hbm, out_hbm,
+    n_gx, n_gy, nodes_ref, w_hbm, src_hbm, out_ref,
     w, src, in_left, in_bottom, out_right, out_top, relay, sig_re, sig_im,
-    w_sem, src_sem, out_sem, send_right, recv_left, send_top, recv_bottom, recv_relay, send_relay,
+    w_sem, src_sem, send_right, recv_left, send_top, recv_bottom, recv_relay, send_relay,
 ):
     gx, gy = lax.axis_index("gx"), lax.axis_index("gy")
     step, order = src.shape[2], src.shape[3]
@@ -249,17 +249,10 @@
 
     lax.fori_loop(1, SECTIONS, section_body, 0)
 
-    def store(side, group):
-        out = out_right if side == 0 else out_top
-        return pltpu.make_async_copy(
-            out.at[SECTIONS - 1, group],
-            out_hbm.at[:, pl.ds(group * step, step), pl.ds(side * edge, edge)],
-            out_sem.at[side, group],
-        )
-
     for group in range(GROUPS):
-        for side in range(2):
-            store(side, group).start()
+        rows = pl.ds(group * step, step)
+        out_ref[:, rows, :edge] = out_right[SECTIONS - 1, group]
+        out_ref[:, rows, edge:] = out_top[SECTIONS - 1, group]
 
     def drain(section, _):
         for group in range(GROUPS):
@@ -277,9 +270,6 @@
         return 0
 
     lax.fori_loop(0, SECTIONS - 1, drain, 0)
-    for group in range(GROUPS):
-        for side in range(2):
-            store(side, group).wait()
 
 
 def solution(mesh):
@@ -294,13 +284,13 @@
         vmem = pltpu.VMEM
         outgoing = pl.pallas_call(
             functools.partial(kernel, n_gx, n_gy),
-            out_shape=jax.ShapeDtypeStruct(source.shape, jnp.bfloat16),
+            out_shape=pltpu.VMEM(source.shape, jnp.bfloat16),
             in_specs=[
                 pl.BlockSpec(memory_space=pltpu.SMEM),
                 pl.BlockSpec(memory_space=pl.ANY),
                 pl.BlockSpec(memory_space=pl.ANY),
             ],
-            out_specs=pl.BlockSpec(memory_space=pl.ANY),
+            out_specs=pl.BlockSpec(memory_space=pltpu.VMEM),
             scratch_shapes=[
                 vmem(weights.shape, jnp.bfloat16),
                 vmem((GROUPS, 2, step, order), jnp.bfloat16),
@@ -313,7 +303,6 @@
                 vmem((GROUPS, step, 128), jnp.float32),
                 dma((2, PIECES)),
                 dma((GROUPS,)),
-                dma((2, GROUPS)),
                 dma((moved, GROUPS)),
                 dma((moved, GROUPS)),
                 dma((moved, GROUPS)),

time: 58.1 us -> 56.6 us (0.974)
  local copies, waits for them, and re-layouts: 1.67 us -> 0.71 us
  Pallas kernels: 56.3 us -> 55.7 us
    unnamed x1, local copies, waits for them, and re-layouts: 1.67 us -> 0.71 us
where the time goes in v3:
time: 56.6 us; the launch traced here: 56.4 us
  Pallas kernels  55.7 us (98%)
  local copies, waits for them, and re-layouts  0.71 us (1%)
    pallas_call x1, Pallas kernels, per_device(): pl.pallas_call(functools.partial(kernel, n_gx, n_gy), out_shape=pltpu.VME...  55.7 us

profile of v3, /device:TPU:212, one launch (start us, length us, event | category | flops | bytes accessed | tf_op | source)
XLA Modules:
  0.0 56.4 jit_solution(4970353354473290897)
XLA Ops:
  0.0 55.7 %shard_map.37 = bf16[2,64,1024]{2,1,0:T(8,128)(2,1)S(1)} custom-call(s32[8]{0:T(128)} %nodes_ref.1, bf16[2,1024,1024]{2,1,0:T(8,128)(2,1)} %bitcast.4, bf16[2,64,1024]{2,1,0:T(8,128)(2,1)} %bitcast.5), custom_call_target="tpu_custom_call" | custom-call | tf_op jit(solution)/shard_map/pallas_call | solution.py:285
  55.7 0.7 %copy.5 = bf16[1,1,2,64,1024]{4,3,2,1,0:T(8,128)(2,1)} copy(bf16[1,1,2,64,1024]{4,3,2,1,0:T(8,128)(2,1)S(1)} %bitcast.3) | data formatting | bytes 524288

commit v4 on v3

--- a/solution.py
+++ b/solution.py
@@ -12,7 +12,7 @@
 SECTIONS = 8
 GROUPS = 4
 PIECES = 4
-PERIOD = 2
+TURNED = (0, 2, 4, 5)
 RELAY_SLOT = (4, 0)
 FIRST_SLOT = (0, 2)
 Y_HI, Y_LO, CORES = 4, 2, 2
@@ -121,10 +121,10 @@
         )
 
     def turned(section):
-        return section % PERIOD == 0
+        return functools.reduce(jnp.logical_or, [section == other for other in TURNED])
 
     def first_group(section):
-        return (section + PERIOD - 1) // PERIOD % GROUPS
+        return sum((section > other).astype(jnp.int32) for other in TURNED) % GROUPS
 
     def send(side, place, section, group):
         if side == 1:

time: 56.6 us -> 55.8 us (0.986)
  the two profiles are of different devices: /device:TPU:212 before, /device:TPU:452 now
where the time goes in v4:
time: 55.8 us; the launch traced here: 55.7 us
  Pallas kernels  55 us (99%)
  local copies, waits for them, and re-layouts  0.71 us (1%)
    pallas_call x1, Pallas kernels, per_device(): pl.pallas_call(functools.partial(kernel, n_gx, n_gy), out_shape=pltpu.VME...  55 us

profile of v4, /device:TPU:452, one launch (start us, length us, event | category | flops | bytes accessed | tf_op | source)
XLA Modules:
  0.0 55.7 jit_solution(4867776585755031947)
XLA Ops:
  0.0 55.0 %shard_map.37 = bf16[2,64,1024]{2,1,0:T(8,128)(2,1)S(1)} custom-call(s32[8]{0:T(128)} %nodes_ref.1, bf16[2,1024,1024]{2,1,0:T(8,128)(2,1)} %bitcast.4, bf16[2,64,1024]{2,1,0:T(8,128)(2,1)} %bitcast.5), custom_call_target="tpu_custom_call" | custom-call | tf_op jit(solution)/shard_map/pallas_call | solution.py:285
  55.0 0.7 %copy.5 = bf16[1,1,2,64,1024]{4,3,2,1,0:T(8,128)(2,1)} copy(bf16[1,1,2,64,1024]{4,3,2,1,0:T(8,128)(2,1)S(1)} %bitcast.3) | data formatting | bytes 524288

commit v5 on v4

--- a/solution.py
+++ b/solution.py
@@ -98,7 +98,7 @@
     def direct(section, group):
         return copy_out(
             out_right, section, group, in_left.at[section, group],
-            send_right, recv_left.at[section, group], (gx + 1, gy),
+            send_right, recv_left.at[section, group], ((gx + 1) % n_gx, gy),
         )
 
     def first_leg(section, group):
@@ -117,7 +117,7 @@
     def upward(section, group):
         return copy_out(
             out_top, section, group, in_bottom.at[section, group],
-            send_top, recv_bottom.at[section, group], (gx, gy + 1),
+            send_top, recv_bottom.at[section, group], (gx, (gy + 1) % n_gy),
         )
 
     def turned(section):

time: 55.8 us -> 56.1 us (level)
  the two profiles are of different devices: /device:TPU:452 before, /device:TPU:454 now
where the time goes in v5:
time: 56.1 us; the launch traced here: 55.9 us
  Pallas kernels  55.2 us (98%)
  local copies, waits for them, and re-layouts  0.71 us (1%)
    pallas_call x1, Pallas kernels, per_device(): pl.pallas_call(functools.partial(kernel, n_gx, n_gy), out_shape=pltpu.VME...  55.2 us

profile of v5, /device:TPU:454, one launch (start us, length us, event | category | flops | bytes accessed | tf_op | source)
XLA Modules:
  0.0 55.9 jit_solution(3654887159715352118)
XLA Ops:
  0.0 55.2 %shard_map.37 = bf16[2,64,1024]{2,1,0:T(8,128)(2,1)S(1)} custom-call(s32[8]{0:T(128)} %nodes_ref.1, bf16[2,1024,1024]{2,1,0:T(8,128)(2,1)} %bitcast.4, bf16[2,64,1024]{2,1,0:T(8,128)(2,1)} %bitcast.5), custom_call_target="tpu_custom_call" | custom-call | tf_op jit(solution)/shard_map/pallas_call | solution.py:285
  55.2 0.7 %copy.5 = bf16[1,1,2,64,1024]{4,3,2,1,0:T(8,128)(2,1)} copy(bf16[1,1,2,64,1024]{4,3,2,1,0:T(8,128)(2,1)S(1)} %bitcast.3) | data formatting | bytes 524288
